TPU v7x, 256 devices: a whole 4x4x8 slice. The times are simulated.
256 devices in a mesh: slab: 32 (over x, z_lo, y), head: 8 (over z_hi, core).
Axes of the slice: x: 4, y: 4, z: 8 (z_hi: 4, z_lo: 2; z = z_hi * 2 + z_lo), core: 2. Of those that a mesh axis runs over, the one named last changes fastest.
Arguments:
- queries: float32 [24576, 2048], P(('slab', 'head')), may hold values from -6 to 6
- key_tokens: float32 [24576, 2048], P(('slab', 'head')), may hold values from -6 to 6
- value_tokens: float32 [24576, 2048], P(('slab', 'head')), may hold values from -6 to 6
- window_reach: int32 [16, 3], replicated, may hold values from 0 to 1, as said below
Outputs:
- attended: float32 [24576, 2048], P(('slab', 'head'))
Inputs may be any that keep to these rules, and one draw needn't show every extreme that they name: `window_reach`: at least one head has reach 1 in all three dimensions and at least one has reach 0 in all three.
All inputs are finite; a program needn't handle non-finite values.
Results may differ from a plain program's by a relative error of at most 0.0003.
Values sent between devices are 32-bit elements; how exact they have to be, the bound alone decides.
No kernel may reach another device: no remote copies, remote signals or barrier semaphores. Data moves between devices by JAX's collectives and lax.ppermute only.
A program may use at most 128 MiB of HBM per device.

v0:
```python
import functools

import jax
import jax.numpy as jnp
import numpy as np
from jax import lax
from jax.experimental import pallas as pl
from jax.experimental.pallas import tpu as pltpu
from jax.sharding import Mesh, PartitionSpec as P

HD = 128
HEADS = 16
BLOCK = 96
TILE_SEG = 192
ROW = 384
KEYS = 768
Q_SCALE = float(HD**-0.5 * np.log2(np.e))
LOW = -1e30
COST = 16 * 10**9

AXES = ("x", "zl", "yh", "yl", "zh", "core")
SIZES = (4, 2, 2, 2, 4, 2)
GROUP = ("zl", "yl", "zh")

OWN_ROWS = ((0, 0), (0, 1), (1, 0), (1, 1))
HALO_ROWS = ((-1, 0), (-1, 1), (2, 0), (2, 1), (0, 2), (1, 2), (-1, 2), (2, 2))


def split_hi_lo(value):
    hi = value.astype(jnp.bfloat16)
    lo = (value - hi.astype(jnp.float32)).astype(jnp.bfloat16)
    return hi, lo


def dot_nt(a, b):
    return lax.dot_general(a, b, (((1,), (1,)), ((), ())), preferred_element_type=jnp.float32)


def dot_nn(a, b):
    return lax.dot_general(a, b, (((1,), (0,)), ((), ())), preferred_element_type=jnp.float32)


def row_flags(rows, info):
    in_time, in_height, in_width, x, yh = (info[i] for i in range(5))
    one = jnp.int32(1)
    flags = []
    for t, h in rows:
        exists = (x > 0).astype(jnp.int32) if t < 0 else (x < 3).astype(jnp.int32) if t > 1 else one
        of_row = []
        for qt in range(2):
            for qh in range(2):
                near_t = one if t == qt else (in_time if abs(t - qt) == 1 else jnp.int32(0))
                if h == 2:
                    near_h = in_height * (yh == 1 - qh).astype(jnp.int32)
                else:
                    near_h = one if h == qh else in_height
                of_row.append(exists * near_t * near_h)
        flags.append(of_row)
    return flags, in_width


def attention_kernel(rows, sources, first, n_in, info, *refs):
    n_rows = len(rows)
    n_out = 2 if first else 1
    ins, outs, scratch = refs[:n_in], refs[n_in : n_in + n_out], refs[n_in + n_out :]
    (q_f, stage, q_b, k_b, v_b, peak, total, acc, acc_0, stat_0, s_0, s_1, m_0, m_1, a_0, a_1, twos, ones,
     q_sem, sem, state_sem, out_sem) = scratch
    flags, in_width = row_flags(rows, info)
    wide = in_width != 0

    def load_row(row):
        @pl.when(functools.reduce(jnp.maximum, flags[row]) != 0)
        def _():
            for side, src in enumerate(sources(ins, row)):
                pltpu.make_async_copy(src, stage.at[row, side], sem.at[row, side]).start()

    q_copy = pltpu.make_async_copy(ins[0], q_f, q_sem)
    q_copy.start()
    for row in range(n_rows):
        load_row(row)
    if not first:
        loads = [
            pltpu.make_async_copy(ins[1], acc_0, state_sem.at[0]),
            pltpu.make_async_copy(ins[2], stat_0, state_sem.at[1]),
        ]
        for load in loads:
            load.start()

    n_twos = jnp.int32(0)
    n_ones = jnp.int32(0)
    for row in range(n_rows):
        held = jnp.int32(-1)
        begun = jnp.int32(0)
        for i in range(4):
            use = flags[row][i]
            pair = use * (held >= 0).astype(jnp.int32)
            twos[n_twos] = row * 32 + jnp.maximum(held, 0) * 8 + i * 2 + (1 - begun)
            n_twos = n_twos + pair
            begun = jnp.maximum(begun, pair)
            held = jnp.where(use == 0, held, jnp.where(pair == 1, -1, i))
        ones[n_ones] = row * 32 + jnp.maximum(held, 0) * 8 + (1 - begun)
        n_ones = n_ones + (held >= 0).astype(jnp.int32)
    last = twos[jnp.maximum(n_twos - 1, 0)] & -2
    twos[n_twos] = last
    twos[n_twos + 1] = last

    peak[...] = jnp.full(peak.shape, LOW, jnp.float32)
    total[...] = jnp.zeros(total.shape, jnp.float32)
    acc[...] = jnp.zeros(acc.shape, jnp.float32)

    q_copy.wait()
    for i in range(4):
        hi, lo = split_hi_lo(q_f[i] * Q_SCALE)
        q_b[i, :, :HD] = hi
        q_b[i, :, HD:] = lo

    def prepare(entry):
        @pl.when((entry & 1) != 0)
        def _():
            row = entry >> 5
            for side in range(2):
                pltpu.make_async_copy(stage.at[row, side], stage.at[row, side], sem.at[row, side]).wait()
            for side in range(2):
                for z in range(4):
                    dst = pl.ds((z // 2) * ROW + side * TILE_SEG + (z % 2) * BLOCK, BLOCK)
                    hi, lo = split_hi_lo(stage[row, side, z, 0])
                    k_b[row, dst, :HD] = hi
                    k_b[row, dst, HD:] = lo
                    hi, lo = split_hi_lo(stage[row, side, z, 1])
                    v_b[row, dst, :HD] = hi
                    v_b[row, dst, HD:] = lo

    def queries_of(entry, double):
        return ((entry >> 3) & 3, (entry >> 1) & 3) if double else ((entry >> 3) & 3,)

    def score(entry, double, tile, s, top, alpha):
        q0, q1, k0, k1 = tile
        size = q1 - q0
        row = entry >> 5
        parts = queries_of(entry, double)
        q = jnp.concatenate([q_b[i, q0:q1, :] for i in parts], axis=0)
        q = jnp.concatenate([q, q], axis=1)
        best = None
        for c in range(k0, k1, 128 * 3):
            kh = k_b[row, c : c + 384, :HD]
            kl = k_b[row, c : c + 384, HD:]
            x = dot_nt(q, jnp.concatenate([kh, kh, kl, kl], axis=1))
            s[: len(parts) * size, c : c + 384] = x
            for j in range(3):
                part = x[:, j * 128 : (j + 1) * 128]
                best = part if best is None else jnp.maximum(best, part)
        best = jnp.max(best, axis=1, keepdims=True)
        for n, i in enumerate(parts):
            own = slice(n * size, (n + 1) * size)
            old = peak[i, q0:q1, :]
            new = jnp.maximum(old, best[own])
            alpha[own, :] = jnp.exp2(old - new)
            top[own, :] = new
            peak[i, q0:q1, :] = new

    def gather(entry, double, tile, s, top, alpha):
        q0, q1, k0, k1 = tile
        size = q1 - q0
        row = entry >> 5
        parts = queries_of(entry, double)
        every = slice(0, len(parts) * size)
        high = top[every, :]
        part = None
        ps = []
        for c in range(k0, k1, 128):
            p = jnp.exp2(s[every, c : c + 128] - high)
            part = p if part is None else part + p
            ps.append(p)
        ph, pw = split_hi_lo(jnp.concatenate(ps, axis=1))
        v = v_b[row, k0:k1, :]
        pv = dot_nn(jnp.concatenate([ph, pw], axis=1), jnp.concatenate([v, v], axis=0))
        pv = pv[:, :HD] + pv[:, HD:]
        for n, i in enumerate(parts):
            own = slice(n * size, (n + 1) * size)
            scale = alpha[own, :]
            total[i, q0:q1, :] = total[i, q0:q1, :] * scale + part[own]
            acc[i, q0:q1, :] = acc[i, q0:q1, :] * scale + pv[own]

    even, odd = (s_0, m_0, a_0), (s_1, m_1, a_1)
    whole = (0, ROW, 0, KEYS)
    halves = [(w * TILE_SEG, (w + 1) * TILE_SEG, w * ROW, (w + 1) * ROW) for w in range(2)]

    @pl.when(wide & (n_twos > 0))
    def _():
        prepare(twos[0])
        score(twos[0], True, whole, *even)

        def step(g, carry):
            n = 2 * g
            here, then, later = twos[n], twos[n + 1], twos[n + 2]
            prepare(then)
            score(then, True, whole, *odd)
            gather(here, True, whole, *even)

            @pl.when(n + 1 < n_twos)
            def _():
                prepare(later)
                score(later, True, whole, *even)
                gather(then, True, whole, *odd)

            return carry

        lax.fori_loop(0, (n_twos + 1) >> 1, step, 0)

    @pl.when(wide)
    def _():
        def step(n, carry):
            here = ones[n]
            prepare(here)
            score(here, False, whole, *even)
            gather(here, False, whole, *even)
            return carry

        lax.fori_loop(0, n_ones, step, 0)

    @pl.when(jnp.logical_not(wide))
    def _():
        for entries, number, double in ((twos, n_twos, True), (ones, n_ones, False)):

            def step(n, carry):
                here = entries[n]
                prepare(here)
                for half, buffers in zip(halves, (even, odd)):
                    score(here, double, half, *buffers)
                for half, buffers in zip(halves, (even, odd)):
                    gather(here, double, half, *buffers)
                return carry

            lax.fori_loop(0, number, step, 0)

    def out_copies(i):
        if first:
            return [
                pltpu.make_async_copy(acc.at[i], outs[0].at[i], out_sem.at[0, i]),
                pltpu.make_async_copy(stat_0.at[i], outs[1].at[i], out_sem.at[1, i]),
            ]
        return [pltpu.make_async_copy(q_f.at[i], outs[0].at[i], out_sem.at[0, i])]

    if not first:
        for load in loads:
            load.wait()
    for i in range(4):
        weight = jnp.sum(total[i], axis=1, keepdims=True)
        if first:
            lane = lax.broadcasted_iota(jnp.int32, (ROW, HD), 1)
            stat_0[i] = jnp.where(lane < HD // 2, peak[i], weight)
        else:
            old = stat_0[i, :, :1]
            here = peak[i, :, :1]
            high = jnp.maximum(old, here)
            scale_0 = jnp.exp2(old - high)
            scale_1 = jnp.exp2(here - high)
            bottom = stat_0[i, :, HD // 2 : HD // 2 + 1] * scale_0 + weight * scale_1
            q_f[i] = (acc_0[i] * scale_0 + acc[i] * scale_1) / bottom
        for copy in out_copies(i):
            copy.start()
    for i in range(4):
        for copy in out_copies(i):
            copy.wait()


def attention(rows, sources, first, info, *arrays):
    n_rows = len(rows)
    hbm = pl.BlockSpec(memory_space=pl.ANY)
    n_out = 2 if first else 1
    state = pltpu.VMEM((4, ROW, HD), jnp.float32)
    column = pltpu.VMEM((2 * ROW, HD), jnp.float32)
    scores = pltpu.VMEM((2 * ROW, KEYS), jnp.float32)
    return pl.pallas_call(
        functools.partial(attention_kernel, rows, sources, first, len(arrays)),
        out_shape=[jax.ShapeDtypeStruct((4, ROW, HD), jnp.float32)] * n_out,
        in_specs=[pl.BlockSpec(memory_space=pltpu.SMEM)] + [hbm] * len(arrays),
        out_specs=[hbm] * n_out,
        scratch_shapes=[
            state,
            pltpu.VMEM((n_rows, 2, 4, 2, BLOCK, HD), jnp.float32),
            pltpu.VMEM((4, ROW, 2 * HD), jnp.bfloat16),
            pltpu.VMEM((n_rows, KEYS, 2 * HD), jnp.bfloat16),
            pltpu.VMEM((n_rows, KEYS, 2 * HD), jnp.bfloat16),
            state,
            state,
            state,
            state,
            state,
            scores,
            scores,
            column,
            column,
            column,
            column,
            pltpu.SMEM((n_rows * 2 + 2,), jnp.int32),
            pltpu.SMEM((n_rows + 1,), jnp.int32),
            pltpu.SemaphoreType.DMA,
            pltpu.SemaphoreType.DMA((n_rows, 2)),
            pltpu.SemaphoreType.DMA((2,)),
            pltpu.SemaphoreType.DMA((2, 4)),
        ],
        compiler_params=pltpu.CompilerParams(vmem_limit_bytes=48 * 1024 * 1024),
        cost_estimate=pl.CostEstimate(flops=COST, bytes_accessed=8 * 2**20, transcendentals=0),
        name="own_rows" if first else "halo_rows",
    )(info, *arrays)


def own_sources(ins, row):
    t, h = OWN_ROWS[row]
    return [ins[1 + side].at[t, h] for side in range(2)]


def halo_sources(ins, row):
    t, h = HALO_ROWS[row]
    out = []
    for side in range(2):
        xm, xp, y, cm, cp = ins[3 + side * 5 : 8 + side * 5]
        if h < 2:
            out.append(xm.at[h] if t < 0 else xp.at[h])
        else:
            out.append(y.at[t] if t in (0, 1) else (cm if t < 0 else cp))
    return out


def body(queries, key_tokens, value_tokens, window_reach):
    yh = lax.axis_index("yh")
    head = (lax.axis_index("yl") ^ yh) * 8 + lax.axis_index("zl") * 4 + lax.axis_index("zh")
    reach = lax.dynamic_slice_in_dim(window_reach, head, 1, 0)[0]
    info = jnp.concatenate([jnp.minimum(reach, 1), jnp.stack([lax.axis_index("x"), yh])])

    def pieces(tensor):
        cut = tensor.reshape(BLOCK, 2, 2, 4, HD)
        flipped = jnp.where(yh == 1, cut[:, ::-1], cut)
        return flipped.transpose(2, 1, 3, 0, 4).reshape(HEADS, BLOCK, HD)

    def exchange(tensor):
        return lax.all_to_all(tensor, GROUP, split_axis=0, concat_axis=0, tiled=True)

    def swap(tensor):
        return lax.ppermute(tensor, "core", [(0, 1), (1, 0)])

    up = [(i, i + 1) for i in range(3)]
    down = [(i + 1, i) for i in range(3)]
    across = [(i, 3 - i) for i in range(4)]

    both = jnp.stack([pieces(key_tokens), pieces(value_tokens)], axis=1)
    own, to_send, info = lax.optimization_barrier((exchange(both), pieces(queries), info))
    own = own.reshape(2, 2, 4, 2, BLOCK, HD)
    own_q = exchange(to_send).reshape(4, ROW, HD)

    xm = lax.ppermute(own[1], "x", up)
    xp = lax.ppermute(own[0], "x", down)
    edge = lax.dynamic_index_in_dim(own, 1 - yh, 1, keepdims=False)
    y = lax.ppermute(edge, ("yh", "yl"), across)
    edge_up = [(i * 4 + j, (i + 1) * 4 + 3 - j) for i in range(3) for j in range(4)]
    edge_down = [((i + 1) * 4 + j, i * 4 + 3 - j) for i in range(3) for j in range(4)]
    cm = lax.ppermute(edge[1], ("x", "yh", "yl"), edge_up)
    cp = lax.ppermute(edge[0], ("x", "yh", "yl"), edge_down)
    halo = (xm, xp, y, cm, cp)
    state = attention(OWN_ROWS, own_sources, True, info, own_q, own, swap(own))
    state, halo = lax.optimization_barrier((state, halo))
    halo = halo + tuple(swap(part) for part in halo)
    (out,) = attention(HALO_ROWS, halo_sources, False, info, own_q, *state, *halo)
    back = exchange(out.reshape(HEADS, BLOCK, HD)).reshape(2, 2, 4, BLOCK, HD)
    back = jnp.where(yh == 1, back[:, ::-1], back)
    return back.transpose(3, 1, 0, 2, 4).reshape(BLOCK, HEADS * HD)


def solution(mesh):
    fine = Mesh(mesh.devices.reshape(SIZES), AXES)
    spec = P(AXES, None)
    return jax.shard_map(
        body,
        mesh=fine,
        in_specs=(spec, spec, spec, P()),
        out_specs=spec,
        check_vma=False,
    )
```

profile of v0, /device:TPU:10, one launch (start us, length us, event | category | flops | bytes accessed | tf_op | source)
XLA Modules:
  0.0 158.1 jit_solution(13841262935704610545)
XLA Ops:
  0.0 1.7 %reshape.37 = f32[96,2,2,4,128]{4,3,2,1,0:T(4,128)S(1)} reshape(f32[96,2048]{1,0:T(8,128)} %param.5) | data formatting | bytes 1572864 | tf_op jit(solution)/shard_map/reshape | solution.py:333
  1.8 0.5 reshape.38
  2.3 0.4 fusion
  2.7 0.3 copy.5
  3.0 0.3 copy.6
  3.2 1.3 pad_maximum_fusion
  4.5 10.1 %all-to-all-start = ((f32[16,2,96,128]{3,2,1,0:T(8,128)}), f32[16,2,96,128]{3,2,1,0:T(8,128)S(1)}, u32[]{:S(2)}, u32[]{:S(2)}) async-start(f32[16,2,96,128]{3,2,1,0:T(8,128)} %pad_maximum_fusion), calls=%async_computation | async-start | bytes 3145728 | tf_op jit(solution)/shard_map/all_to_all | solution.py:338
  14.6 0.5 reshape.39
  15.1 0.0 copy-start.2
  15.2 0.1 fusion.2
  15.3 1.1 copy.7
  16.4 0.2 minimum_reduce_fusion
  16.6 0.1 pad_add_fusion.info
  16.7 37.4 %all-to-all-done = f32[16,2,96,128]{3,2,1,0:T(8,128)S(1)} async-done(((f32[16,2,96,128]{3,2,1,0:T(8,128)}), f32[16,2,96,128]{3,2,1,0:T(8,128)S(1)}, u32[]{:S(2)}, u32[]{:S(2)}) %all-to-all-start) | async-done | bytes 1572896 | tf_op jit(solution)/shard_map/all_to_all | solution.py:338
  54.0 0.0 collective-permute-start
  54.0 4.5 %all-to-all-start.1 = ((f32[16,96,128]{2,1,0:T(8,128)}), f32[16,96,128]{2,1,0:T(8,128)S(1)}, u32[]{:S(2)}, u32[]{:S(2)}) async-start(f32[16,96,128]{2,1,0:T(8,128)} %bitcast.5), calls=%async_computation.1 | async-start | bytes 1572864 | tf_op jit(solution)/shard_map/all_to_all | solution.py:338
  58.5 0.9 dynamic-slice_bitcast_fusion.1
  59.5 2.8 %collective-permute-start.5 = (f32[4,2,96,128]{3,2,1,0:T(8,128)}, f32[4,2,96,128]{3,2,1,0:T(8,128)S(1)}, u32[]{:S(2)}, u32[]{:S(2)}) collective-permute-start(f32[4,2,96,128]{3,2,1,0:T(8,128)} %get-tuple-element.29), channel_id=1, source_target_pairs={{64,24},{72,16},{80,8},{88,0},{128,88},{136,80},{144,72},{152,64},... | collective-permute-start | bytes 1179656 | tf_op jit(solution)/shard_map/ppermute | solution.py:359
  62.3 3.9 %collective-permute-start.4 = (f32[4,2,96,128]{3,2,1,0:T(8,128)}, f32[4,2,96,128]{3,2,1,0:T(8,128)}, u32[]{:S(2)}, u32[]{:S(2)}) collective-permute-start(f32[4,2,96,128]{3,2,1,0:T(8,128)} %get-tuple-element.30), channel_id=1, source_target_pairs={{0,88},{8,80},{16,72},{24,64},{64,152},{72,144},{80,136},{88,128},... | collective-permute-start | bytes 1179656 | tf_op jit(solution)/shard_map/ppermute | solution.py:358
  66.2 1.0 dynamic-slice_bitcast_fusion
  67.2 0.9 collective-permute-start.3
  68.1 1.3 fusion.4
  69.4 3.4 %collective-permute-start.1 = (f32[2,4,2,96,128]{4,3,2,1,0:T(8,128)}, f32[2,4,2,96,128]{4,3,2,1,0:T(8,128)S(1)}, u32[]{:S(2)}, u32[]{:S(2)}) collective-permute-start(f32[2,4,2,96,128]{4,3,2,1,0:T(8,128)} %bitcast.10), channel_id=1, source_target_pairs={{0,64},{64,128},{128,192},{1,65},{65,129},{129,193},{2,66},{66,130... | collective-permute-start | bytes 2359304 | tf_op jit(solution)/shard_map/ppermute | solution.py:352
  72.9 0.0 collective-permute-done.refs_2_
  72.9 2.5 %collective-permute-start.2 = (f32[2,4,2,96,128]{4,3,2,1,0:T(8,128)}, f32[2,4,2,96,128]{4,3,2,1,0:T(8,128)}, u32[]{:S(2)}, u32[]{:S(2)}) collective-permute-start(f32[2,4,2,96,128]{4,3,2,1,0:T(8,128)} %bitcast.11), channel_id=1, source_target_pairs={{64,0},{128,64},{192,128},{65,1},{129,65},{193,129},{66,2},{130,66... | collective-permute-start | bytes 2359304 | tf_op jit(solution)/shard_map/ppermute | solution.py:353
  75.4 6.4 %all-to-all-done.1 = f32[16,96,128]{2,1,0:T(8,128)S(1)} async-done(((f32[16,96,128]{2,1,0:T(8,128)}), f32[16,96,128]{2,1,0:T(8,128)S(1)}, u32[]{:S(2)}, u32[]{:S(2)}) %all-to-all-start.1) | async-done | bytes 786464 | tf_op jit(solution)/shard_map/all_to_all | solution.py:338
  81.7 13.0 %own_rows.1 = (f32[4,384,128]{2,1,0:T(8,128)S(1)}, f32[4,384,128]{2,1,0:T(8,128)S(1)}) custom-call(s32[5]{0:T(128)S(1)} %pad_add_fusion.info, f32[4,384,128]{2,1,0:T(8,128)S(1)} %bitcast.29, f32[2,2,4,2,96,128]{5,4,3,2,1,0:T(8,128)S(1)} %bitcast.28, f32[2,2,4,2,96,128]{5,4,3,2,1,0:T(8,128)} %collective-permute-done.refs_2_), custom_call_target="tpu_custom_call" | custom-call | flops 16000000000 | bytes 8388608 | tf_op jit(solution)/shard_map/own_rows/pallas_call | solution.py:274
  94.8 0.0 collective-permute-done.5.refs_7_
  94.8 4.0 %collective-permute-done.3.refs_5_ = f32[2,4,2,96,128]{4,3,2,1,0:T(8,128)} collective-permute-done((f32[2,4,2,96,128]{4,3,2,1,0:T(8,128)}, f32[2,4,2,96,128]{4,3,2,1,0:T(8,128)}, u32[]{:S(2)}, u32[]{:S(2)}) %collective-permute-start.3) | collective-permute-done | bytes 786464 | tf_op jit(solution)/shard_map/ppermute | solution.py:355
  98.8 0.0 collective-permute-done.1.refs_3_
  98.8 0.0 collective-permute-done.2.refs_4_
  98.8 0.0 collective-permute-start.6
  98.8 0.5 collective-permute-start.7
  99.3 0.1 collective-permute-start.8
  99.4 0.4 collective-permute-start.9
  99.8 0.1 collective-permute-start.10
  99.9 4.8 %collective-permute-done.9.refs_11_ = f32[4,2,96,128]{3,2,1,0:T(8,128)S(1)} collective-permute-done((f32[4,2,96,128]{3,2,1,0:T(8,128)}, f32[4,2,96,128]{3,2,1,0:T(8,128)S(1)}, u32[]{:S(2)}, u32[]{:S(2)}) %collective-permute-start.9) | collective-permute-done | bytes 393248 | tf_op jit(solution)/shard_map/ppermute | solution.py:341
  104.7 0.0 collective-permute-done.10.refs_12_
  104.7 0.0 collective-permute-done.6.refs_8_
  104.7 0.0 collective-permute-done.8.refs_10_
  104.7 0.8 copy-done.3
  105.6 0.3 copy-done.4
  105.8 0.9 copy-done.5
  106.7 8.2 %halo_rows.1 = f32[4,384,128]{2,1,0:T(8,128)S(1)} custom-call(s32[5]{0:T(128)S(1)} %pad_add_fusion.info, f32[4,384,128]{2,1,0:T(8,128)S(1)} %bitcast.30, f32[4,384,128]{2,1,0:T(8,128)S(1)} %get-tuple-element.22.refs_1_, f32[4,384,128]{2,1,0:T(8,128)S(1)} %get-tuple-element.23.refs_2_, f32[2,4,2,96,128]{4,3,2,1,0:T(8,128)S(1)} %collective-permute-done.1.refs_3_, ...), custom_call_target="tpu_custom_call" | custom-call | flops 16000000000 | bytes 8388608 | tf_op jit(solution)/shard_map/halo_rows/pallas_call | solution.py:274
  115.0 41.3 %all_to_all.15 = f32[16,96,128]{2,1,0:T(8,128)S(1)} all-to-all(f32[16,96,128]{2,1,0:T(8,128)S(1)} %bitcast.31), channel_id=1, replica_groups=mesh['x'=4,'zl'=2,'yh'=2,'yl'=2,'zh'=4,'core'=2] {'zl','yl','zh'}, dimensions={0} | all-to-all | bytes 1572864 | tf_op jit(solution)/shard_map/all_to_all | solution.py:338
  156.3 0.5 copy.8
  156.8 0.1 fusion.3
  157.0 1.2 reshape.45
  (10 shorter events, 0.0 us)
Async XLA Ops:
  0.0 1.7 %copy-start = (f32[96,2048]{1,0:T(8,128)S(1)}, f32[96,2048]{1,0:T(8,128)}, u32[]{:S(2)}) copy-start(f32[96,2048]{1,0:T(8,128)} %param.6) | copy-start | bytes 2359300
  4.5 10.1 %copy-start.1 = (f32[96,2048]{1,0:T(8,128)S(1)}, f32[96,2048]{1,0:T(8,128)}, u32[]{:S(2)}) copy-start(f32[96,2048]{1,0:T(8,128)} %param.4) | copy-start | bytes 2359300
  4.5 49.5 %all-to-all-start = ((f32[16,2,96,128]{3,2,1,0:T(8,128)}), f32[16,2,96,128]{3,2,1,0:T(8,128)S(1)}, u32[]{:S(2)}, u32[]{:S(2)}) async-start(f32[16,2,96,128]{3,2,1,0:T(8,128)} %pad_maximum_fusion), calls=%async_computation | async-start | bytes 3145728 | tf_op jit(solution)/shard_map/all_to_all | solution.py:338
  15.1 1.3 copy-start.2
  54.0 18.8 %collective-permute-start = (f32[2,2,4,2,96,128]{5,4,3,2,1,0:T(8,128)S(1)}, f32[2,2,4,2,96,128]{5,4,3,2,1,0:T(8,128)}, u32[]{:S(2)}, u32[]{:S(2)}) collective-permute-start(f32[2,2,4,2,96,128]{5,4,3,2,1,0:T(8,128)S(1)} %bitcast.25), channel_id=1, source_target_pairs={{0,1},{1,0},{2,3},{3,2},{4,5},{5,4},{6,7},{7,6},{8,9},{9,8},{10,11... | collective-permute-start | bytes 4718600 | tf_op jit(solution)/shard_map/ppermute | solution.py:341
  54.0 27.7 %all-to-all-start.1 = ((f32[16,96,128]{2,1,0:T(8,128)}), f32[16,96,128]{2,1,0:T(8,128)S(1)}, u32[]{:S(2)}, u32[]{:S(2)}) async-start(f32[16,96,128]{2,1,0:T(8,128)} %bitcast.5), calls=%async_computation.1 | async-start | bytes 1572864 | tf_op jit(solution)/shard_map/all_to_all | solution.py:338
  59.5 35.3 %collective-permute-start.5 = (f32[4,2,96,128]{3,2,1,0:T(8,128)}, f32[4,2,96,128]{3,2,1,0:T(8,128)S(1)}, u32[]{:S(2)}, u32[]{:S(2)}) collective-permute-start(f32[4,2,96,128]{3,2,1,0:T(8,128)} %get-tuple-element.29), channel_id=1, source_target_pairs={{64,24},{72,16},{80,8},{88,0},{128,88},{136,80},{144,72},{152,64},... | collective-permute-start | bytes 1179656 | tf_op jit(solution)/shard_map/ppermute | solution.py:359
  62.3 32.5 %collective-permute-start.4 = (f32[4,2,96,128]{3,2,1,0:T(8,128)}, f32[4,2,96,128]{3,2,1,0:T(8,128)}, u32[]{:S(2)}, u32[]{:S(2)}) collective-permute-start(f32[4,2,96,128]{3,2,1,0:T(8,128)} %get-tuple-element.30), channel_id=1, source_target_pairs={{0,88},{8,80},{16,72},{24,64},{64,152},{72,144},{80,136},{88,128},... | collective-permute-start | bytes 1179656 | tf_op jit(solution)/shard_map/ppermute | solution.py:358
  67.2 31.6 %collective-permute-start.3 = (f32[2,4,2,96,128]{4,3,2,1,0:T(8,128)}, f32[2,4,2,96,128]{4,3,2,1,0:T(8,128)}, u32[]{:S(2)}, u32[]{:S(2)}) collective-permute-start(f32[2,4,2,96,128]{4,3,2,1,0:T(8,128)} %dynamic-slice_bitcast_fusion), channel_id=1, source_target_pairs={{0,24},{8,16},{16,8},{24,0},{1,25},{9,17},{17,9},{25,1},{2,26},{10... | collective-permute-start | bytes 2359304 | tf_op jit(solution)/shard_map/ppermute | solution.py:355
  69.4 29.3 %collective-permute-start.1 = (f32[2,4,2,96,128]{4,3,2,1,0:T(8,128)}, f32[2,4,2,96,128]{4,3,2,1,0:T(8,128)S(1)}, u32[]{:S(2)}, u32[]{:S(2)}) collective-permute-start(f32[2,4,2,96,128]{4,3,2,1,0:T(8,128)} %bitcast.10), channel_id=1, source_target_pairs={{0,64},{64,128},{128,192},{1,65},{65,129},{129,193},{2,66},{66,130... | collective-permute-start | bytes 2359304 | tf_op jit(solution)/shard_map/ppermute | solution.py:352
  72.9 25.9 %collective-permute-start.2 = (f32[2,4,2,96,128]{4,3,2,1,0:T(8,128)}, f32[2,4,2,96,128]{4,3,2,1,0:T(8,128)}, u32[]{:S(2)}, u32[]{:S(2)}) collective-permute-start(f32[2,4,2,96,128]{4,3,2,1,0:T(8,128)} %bitcast.11), channel_id=1, source_target_pairs={{64,0},{128,64},{192,128},{65,1},{129,65},{193,129},{66,2},{130,66... | collective-permute-start | bytes 2359304 | tf_op jit(solution)/shard_map/ppermute | solution.py:353
  98.8 5.9 %collective-permute-start.6 = (f32[2,4,2,96,128]{4,3,2,1,0:T(8,128)S(1)}, f32[2,4,2,96,128]{4,3,2,1,0:T(8,128)S(1)}, u32[]{:S(2)}, u32[]{:S(2)}) collective-permute-start(f32[2,4,2,96,128]{4,3,2,1,0:T(8,128)S(1)} %collective-permute-done.1.refs_3_), channel_id=1, source_target_pairs={{0,1},{1,0},{2,3},{3,2},{4,5},{5,4},{6,7},{7,6},{8,9},{9,8},{10,11... | collective-permute-start | bytes 2359304 | tf_op jit(solution)/shard_map/ppermute | solution.py:341
  98.8 5.9 %collective-permute-start.7 = (f32[2,4,2,96,128]{4,3,2,1,0:T(8,128)}, f32[2,4,2,96,128]{4,3,2,1,0:T(8,128)S(1)}, u32[]{:S(2)}, u32[]{:S(2)}) collective-permute-start(f32[2,4,2,96,128]{4,3,2,1,0:T(8,128)} %collective-permute-done.2.refs_4_), channel_id=1, source_target_pairs={{0,1},{1,0},{2,3},{3,2},{4,5},{5,4},{6,7},{7,6},{8,9},{9,8},{10,11... | collective-permute-start | bytes 2359304 | tf_op jit(solution)/shard_map/ppermute | solution.py:341
  99.3 5.4 %collective-permute-start.8 = (f32[2,4,2,96,128]{4,3,2,1,0:T(8,128)}, f32[2,4,2,96,128]{4,3,2,1,0:T(8,128)S(1)}, u32[]{:S(2)}, u32[]{:S(2)}) collective-permute-start(f32[2,4,2,96,128]{4,3,2,1,0:T(8,128)} %collective-permute-done.3.refs_5_), channel_id=1, source_target_pairs={{0,1},{1,0},{2,3},{3,2},{4,5},{5,4},{6,7},{7,6},{8,9},{9,8},{10,11... | collective-permute-start | bytes 2359304 | tf_op jit(solution)/shard_map/ppermute | solution.py:341
  99.4 5.3 %collective-permute-start.9 = (f32[4,2,96,128]{3,2,1,0:T(8,128)}, f32[4,2,96,128]{3,2,1,0:T(8,128)S(1)}, u32[]{:S(2)}, u32[]{:S(2)}) collective-permute-start(f32[4,2,96,128]{3,2,1,0:T(8,128)} %collective-permute-done.4.refs_6_), channel_id=1, source_target_pairs={{0,1},{1,0},{2,3},{3,2},{4,5},{5,4},{6,7},{7,6},{8,9},{9,8},{10,11... | collective-permute-start | bytes 1179656 | tf_op jit(solution)/shard_map/ppermute | solution.py:341
  99.8 4.9 %collective-permute-start.10 = (f32[4,2,96,128]{3,2,1,0:T(8,128)S(1)}, f32[4,2,96,128]{3,2,1,0:T(8,128)S(1)}, u32[]{:S(2)}, u32[]{:S(2)}) collective-permute-start(f32[4,2,96,128]{3,2,1,0:T(8,128)S(1)} %collective-permute-done.5.refs_7_), channel_id=1, source_target_pairs={{0,1},{1,0},{2,3},{3,2},{4,5},{5,4},{6,7},{7,6},{8,9},{9,8},{10,11... | collective-permute-start | bytes 1179656 | tf_op jit(solution)/shard_map/ppermute | solution.py:341
  104.7 0.9 copy-start.3
  104.7 1.1 copy-start.4
  105.8 0.9 copy-start.5
where the time goes:
time: 160 us; the launch traced here: 158 us
  waiting for transfers between devices  52.5 us (33%)
  blocking collectives  41.3 us (26%)
  starting transfers between devices  29.2 us (18%)
  Pallas kernels  21.3 us (13%)
  local copies, waits for them, and re-layouts  11.4 us (7%)
  other arithmetic  2.24 us (1%)
    all_to_all x2, waiting for transfers between devices, exchange(): lax.all_to_all(tensor, GROUP, split_axis=0, concat_axis=0, tiled=True)  43.7 us
    all_to_all x1, blocking collectives, exchange(): lax.all_to_all(tensor, GROUP, split_axis=0, concat_axis=0, tiled=True)  41.3 us
    pallas_call x2, Pallas kernels, attention(): pl.pallas_call(functools.partial(attention_kernel, rows, sources, first,...  21.3 us
    all_to_all x2, starting transfers between devices, exchange(): lax.all_to_all(tensor, GROUP, split_axis=0, concat_axis=0, tiled=True)  14.5 us
    ppermute x6, waiting for transfers between devices, swap(): return lax.ppermute(tensor, 'core', [(0, 1), (1, 0)])  4.77 us
    ppermute x1, waiting for transfers between devices, body(): y = lax.ppermute(edge, ('yh', 'yl'), across)  4 us
    ppermute x1, starting transfers between devices, body(): cm = lax.ppermute(edge[1], ('x', 'yh', 'yl'), edge_up)  3.92 us
    ppermute x1, starting transfers between devices, body(): xm = lax.ppermute(own[1], 'x', up)  3.41 us
  transfers between devices with their start and end apart: 13, of which 4 were waited for; matrix products, arithmetic and copies ran while one was open for 3% of the time, Pallas kernels for 8%

commit v1 on v0

--- a/solution.py
+++ b/solution.py
@@ -63,21 +63,13 @@
     n_rows = len(rows)
     n_out = 2 if first else 1
     ins, outs, scratch = refs[:n_in], refs[n_in : n_in + n_out], refs[n_in + n_out :]
-    (q_f, stage, q_b, k_b, v_b, peak, total, acc, acc_0, stat_0, s_0, s_1, m_0, m_1, a_0, a_1, twos, ones,
-     q_sem, sem, state_sem, out_sem) = scratch
+    (q_f, q_b, k_b, v_b, peak, total, acc, acc_0, stat_0, s_0, s_1, m_0, m_1, a_0, a_1, twos, ones,
+     q_sem, state_sem, out_sem) = scratch
     flags, in_width = row_flags(rows, info)
     wide = in_width != 0
 
-    def load_row(row):
-        @pl.when(functools.reduce(jnp.maximum, flags[row]) != 0)
-        def _():
-            for side, src in enumerate(sources(ins, row)):
-                pltpu.make_async_copy(src, stage.at[row, side], sem.at[row, side]).start()
-
     q_copy = pltpu.make_async_copy(ins[0], q_f, q_sem)
     q_copy.start()
-    for row in range(n_rows):
-        load_row(row)
     if not first:
         loads = [
             pltpu.make_async_copy(ins[1], acc_0, state_sem.at[0]),
@@ -118,17 +110,19 @@
         @pl.when((entry & 1) != 0)
         def _():
             row = entry >> 5
-            for side in range(2):
-                pltpu.make_async_copy(stage.at[row, side], stage.at[row, side], sem.at[row, side]).wait()
-            for side in range(2):
-                for z in range(4):
-                    dst = pl.ds((z // 2) * ROW + side * TILE_SEG + (z % 2) * BLOCK, BLOCK)
-                    hi, lo = split_hi_lo(stage[row, side, z, 0])
-                    k_b[row, dst, :HD] = hi
-                    k_b[row, dst, HD:] = lo
-                    hi, lo = split_hi_lo(stage[row, side, z, 1])
-                    v_b[row, dst, :HD] = hi
-                    v_b[row, dst, HD:] = lo
+            for r in range(n_rows):
+
+                @pl.when(row == r)
+                def _():
+                    for side, src in enumerate(sources(ins, r)):
+                        for z in range(4):
+                            start = (z // 2) * ROW + side * TILE_SEG + (z % 2) * BLOCK
+                            hi, lo = split_hi_lo(src[z, 0])
+                            k_b[r, start : start + BLOCK, :HD] = hi
+                            k_b[r, start : start + BLOCK, HD:] = lo
+                            hi, lo = split_hi_lo(src[z, 1])
+                            v_b[r, start : start + BLOCK, :HD] = hi
+                            v_b[r, start : start + BLOCK, HD:] = lo
 
     def queries_of(entry, double):
         return ((entry >> 3) & 3, (entry >> 1) & 3) if double else ((entry >> 3) & 3,)
@@ -274,11 +268,12 @@
     return pl.pallas_call(
         functools.partial(attention_kernel, rows, sources, first, len(arrays)),
         out_shape=[jax.ShapeDtypeStruct((4, ROW, HD), jnp.float32)] * n_out,
-        in_specs=[pl.BlockSpec(memory_space=pltpu.SMEM)] + [hbm] * len(arrays),
+        in_specs=[pl.BlockSpec(memory_space=pltpu.SMEM)]
+        + [hbm] * (1 if first else 3)
+        + [pl.BlockSpec(memory_space=pltpu.VMEM)] * (len(arrays) - (1 if first else 3)),
         out_specs=[hbm] * n_out,
         scratch_shapes=[
             state,
-            pltpu.VMEM((n_rows, 2, 4, 2, BLOCK, HD), jnp.float32),
             pltpu.VMEM((4, ROW, 2 * HD), jnp.bfloat16),
             pltpu.VMEM((n_rows, KEYS, 2 * HD), jnp.bfloat16),
             pltpu.VMEM((n_rows, KEYS, 2 * HD), jnp.bfloat16),
@@ -296,14 +291,13 @@
             pltpu.SMEM((n_rows * 2 + 2,), jnp.int32),
             pltpu.SMEM((n_rows + 1,), jnp.int32),
             pltpu.SemaphoreType.DMA,
-            pltpu.SemaphoreType.DMA((n_rows, 2)),
             pltpu.SemaphoreType.DMA((2,)),
             pltpu.SemaphoreType.DMA((2, 4)),
         ],
-        compiler_params=pltpu.CompilerParams(vmem_limit_bytes=48 * 1024 * 1024),
+        compiler_params=pltpu.CompilerParams(vmem_limit_bytes=(24 if first else 28) * 1024 * 1024),
         cost_estimate=pl.CostEstimate(flops=COST, bytes_accessed=8 * 2**20, transcendentals=0),
         name="own_rows" if first else "halo_rows",
-    )(info, *arrays)
+    )(info, *arrays[: 1 if first else 3], *[pltpu.with_memory_space_constraint(x, pltpu.VMEM) for x in arrays[1 if first else 3 :]])
 
 
 def own_sources(ins, row):

time: 160 us -> 158 us (0.988); the launches traced: 158 us -> 158 us
  Pallas kernels: 21.3 us -> 40.8 us
  blocking collectives: 41.3 us -> 27.8 us
  waiting for transfers between devices: 52.5 us -> 47.7 us
  local copies, waits for them, and re-layouts: 11.4 us -> 9.39 us
    pallas_call x2, Pallas kernels: 21.3 us -> 40.8 us  [attention(): pl.pallas_call(functools.partial(attention_kernel, rows, sources, first,...]
    all_to_all x1, blocking collectives: 41.3 us -> 27.8 us  [exchange(): lax.all_to_all(tensor, GROUP, split_axis=0, concat_axis=0, tiled=True)]
    ppermute x1, waiting for transfers between devices: 4 us -> 0.01 us  [body(): y = lax.ppermute(edge, ('yh', 'yl'), across)]
    unnamed x12 -> x6, local copies, waits for them, and re-layouts: 2.04 us -> 0.01 us
  transfers between devices with their start and end apart: 13 -> 13, of which waited for: 4 -> 3; matrix products, arithmetic and copies ran while one was open for 3% -> 3% of each run, Pallas kernels for 8% -> 13%
where the time goes in v1:
time: 158 us
  waiting for transfers between devices  47.7 us (30%)
  Pallas kernels  40.8 us (26%)
  starting transfers between devices  30.1 us (19%)
  blocking collectives  27.8 us (18%)
  local copies, waits for them, and re-layouts  9.39 us (6%)
  other arithmetic  2.25 us (1%)
    all_to_all x2, waiting for transfers between devices, exchange(): lax.all_to_all(tensor, GROUP, split_axis=0, concat_axis=0, tiled=True)  42.9 us
    pallas_call x2, Pallas kernels, attention(): pl.pallas_call(functools.partial(attention_kernel, rows, sources, first,...  40.8 us
    all_to_all x1, blocking collectives, exchange(): lax.all_to_all(tensor, GROUP, split_axis=0, concat_axis=0, tiled=True)  27.8 us
    all_to_all x2, starting transfers between devices, exchange(): lax.all_to_all(tensor, GROUP, split_axis=0, concat_axis=0, tiled=True)  14.5 us
    ppermute x6, waiting for transfers between devices, swap(): return lax.ppermute(tensor, 'core', [(0, 1), (1, 0)])  4.76 us
    ppermute x1, starting transfers between devices, body(): cm = lax.ppermute(edge[1], ('x', 'yh', 'yl'), edge_up)  3.92 us
    ppermute x1, starting transfers between devices, body(): xm = lax.ppermute(own[1], 'x', up)  3.41 us
    ppermute x1, starting transfers between devices, body(): xp = lax.ppermute(own[0], 'x', down)  3.28 us
  transfers between devices with their start and end apart: 13, of which 3 were waited for; matrix products, arithmetic and copies ran while one was open for 3% of the time, Pallas kernels for 13%

profile of v1, /device:TPU:10, one launch (start us, length us, event | category | flops | bytes accessed | tf_op | source)
XLA Modules:
  0.0 158.3 jit_solution(17535337633806192360)
XLA Ops:
  0.0 1.7 %reshape.37 = f32[96,2,2,4,128]{4,3,2,1,0:T(4,128)S(1)} reshape(f32[96,2048]{1,0:T(8,128)} %param.5) | data formatting | bytes 1572864 | tf_op jit(solution)/shard_map/reshape | solution.py:327
  1.8 0.5 reshape.38
  2.3 0.4 fusion
  2.7 0.3 copy.5
  3.0 0.3 copy.6
  3.2 1.3 pad_maximum_fusion
  4.5 10.1 %all-to-all-start = ((f32[16,2,96,128]{3,2,1,0:T(8,128)}), f32[16,2,96,128]{3,2,1,0:T(8,128)S(1)}, u32[]{:S(2)}, u32[]{:S(2)}) async-start(f32[16,2,96,128]{3,2,1,0:T(8,128)} %pad_maximum_fusion), calls=%async_computation | async-start | bytes 3145728 | tf_op jit(solution)/shard_map/all_to_all | solution.py:332
  14.6 0.0 copy-done.1
  14.6 0.5 reshape.39
  15.2 0.0 copy-start.2
  15.2 0.1 fusion.2
  15.3 1.1 copy.7
  16.4 0.2 minimum_reduce_fusion
  16.6 0.1 pad_add_fusion.info
  16.7 37.4 %all-to-all-done = f32[16,2,96,128]{3,2,1,0:T(8,128)S(1)} async-done(((f32[16,2,96,128]{3,2,1,0:T(8,128)}), f32[16,2,96,128]{3,2,1,0:T(8,128)S(1)}, u32[]{:S(2)}, u32[]{:S(2)}) %all-to-all-start) | async-done | bytes 1572896 | tf_op jit(solution)/shard_map/all_to_all | solution.py:332
  54.1 0.0 collective-permute-start
  54.1 4.5 %all-to-all-start.1 = ((f32[16,96,128]{2,1,0:T(8,128)}), f32[16,96,128]{2,1,0:T(8,128)S(1)}, u32[]{:S(2)}, u32[]{:S(2)}) async-start(f32[16,96,128]{2,1,0:T(8,128)} %bitcast.5), calls=%async_computation.1 | async-start | bytes 1572864 | tf_op jit(solution)/shard_map/all_to_all | solution.py:332
  58.5 1.0 dynamic-slice_bitcast_fusion.1
  59.5 2.8 %collective-permute-start.5 = (f32[4,2,96,128]{3,2,1,0:T(8,128)}, f32[4,2,96,128]{3,2,1,0:T(8,128)S(1)}, u32[]{:S(2)}, u32[]{:S(2)}) collective-permute-start(f32[4,2,96,128]{3,2,1,0:T(8,128)} %get-tuple-element.29), channel_id=1, source_target_pairs={{64,24},{72,16},{80,8},{88,0},{128,88},{136,80},{144,72},{152,64},... | collective-permute-start | bytes 1179656 | tf_op jit(solution)/shard_map/ppermute | solution.py:353
  62.3 3.9 %collective-permute-start.4 = (f32[4,2,96,128]{3,2,1,0:T(8,128)}, f32[4,2,96,128]{3,2,1,0:T(8,128)}, u32[]{:S(2)}, u32[]{:S(2)}) collective-permute-start(f32[4,2,96,128]{3,2,1,0:T(8,128)} %get-tuple-element.30), channel_id=1, source_target_pairs={{0,88},{8,80},{16,72},{24,64},{64,152},{72,144},{80,136},{88,128},... | collective-permute-start | bytes 1179656 | tf_op jit(solution)/shard_map/ppermute | solution.py:352
  66.2 1.0 dynamic-slice_bitcast_fusion
  67.2 0.9 collective-permute-start.3
  68.2 1.3 fusion.4
  69.5 3.4 %collective-permute-start.1 = (f32[2,4,2,96,128]{4,3,2,1,0:T(8,128)}, f32[2,4,2,96,128]{4,3,2,1,0:T(8,128)}, u32[]{:S(2)}, u32[]{:S(2)}) collective-permute-start(f32[2,4,2,96,128]{4,3,2,1,0:T(8,128)} %bitcast.10), channel_id=1, source_target_pairs={{0,64},{64,128},{128,192},{1,65},{65,129},{129,193},{2,66},{66,130... | collective-permute-start | bytes 2359304 | tf_op jit(solution)/shard_map/ppermute | solution.py:346
  72.9 0.0 collective-permute-done.refs_2_
  72.9 3.3 %collective-permute-start.2 = (f32[2,4,2,96,128]{4,3,2,1,0:T(8,128)}, f32[2,4,2,96,128]{4,3,2,1,0:T(8,128)}, u32[]{:S(2)}, u32[]{:S(2)}) collective-permute-start(f32[2,4,2,96,128]{4,3,2,1,0:T(8,128)} %bitcast.11), channel_id=1, source_target_pairs={{64,0},{128,64},{192,128},{65,1},{129,65},{193,129},{66,2},{130,66... | collective-permute-start | bytes 2359304 | tf_op jit(solution)/shard_map/ppermute | solution.py:347
  76.2 5.6 %all-to-all-done.1 = f32[16,96,128]{2,1,0:T(8,128)S(1)} async-done(((f32[16,96,128]{2,1,0:T(8,128)}), f32[16,96,128]{2,1,0:T(8,128)S(1)}, u32[]{:S(2)}, u32[]{:S(2)}) %all-to-all-start.1) | async-done | bytes 786464 | tf_op jit(solution)/shard_map/all_to_all | solution.py:332
  81.7 19.9 %own_rows.1 = (f32[4,384,128]{2,1,0:T(8,128)S(1)}, f32[4,384,128]{2,1,0:T(8,128)S(1)}) custom-call(s32[5]{0:T(128)S(1)} %pad_add_fusion.info, f32[4,384,128]{2,1,0:T(8,128)S(1)} %bitcast.29, f32[2,2,4,2,96,128]{5,4,3,2,1,0:T(8,128)S(1)} %bitcast.28, f32[2,2,4,2,96,128]{5,4,3,2,1,0:T(8,128)} %collective-permute-done.refs_2_), custom_call_target="tpu_custom_call" | custom-call | flops 16000000000 | bytes 8388608 | tf_op jit(solution)/shard_map/own_rows/pallas_call | solution.py:268
  101.6 0.0 collective-permute-done.5.refs_7_
  101.6 0.0 collective-permute-done.4.refs_6_
  101.6 0.0 collective-permute-done.3.refs_5_
  101.6 0.0 collective-permute-done.1.refs_3_
  101.6 0.0 collective-permute-done.2.refs_4_
  101.7 0.1 collective-permute-start.6
  101.8 0.5 collective-permute-start.7
  102.2 0.1 collective-permute-start.8
  102.3 0.4 collective-permute-start.9
  102.8 0.1 collective-permute-start.10
  102.9 4.7 %collective-permute-done.9.refs_11_ = f32[4,2,96,128]{3,2,1,0:T(8,128)S(1)} collective-permute-done((f32[4,2,96,128]{3,2,1,0:T(8,128)}, f32[4,2,96,128]{3,2,1,0:T(8,128)S(1)}, u32[]{:S(2)}, u32[]{:S(2)}) %collective-permute-start.9) | collective-permute-done | bytes 393248 | tf_op jit(solution)/shard_map/ppermute | solution.py:335
  107.6 0.0 collective-permute-done.10.refs_12_
  107.6 0.0 collective-permute-done.6.refs_8_
  107.6 0.0 collective-permute-done.7.refs_9_
  107.6 0.0 collective-permute-done.8.refs_10_
  107.6 20.9 %halo_rows.1 = f32[4,384,128]{2,1,0:T(8,128)S(1)} custom-call(s32[5]{0:T(128)S(1)} %pad_add_fusion.info, f32[4,384,128]{2,1,0:T(8,128)S(1)} %bitcast.30, f32[4,384,128]{2,1,0:T(8,128)S(1)} %get-tuple-element.22.refs_1_, f32[4,384,128]{2,1,0:T(8,128)S(1)} %get-tuple-element.23.refs_2_, f32[2,4,2,96,128]{4,3,2,1,0:T(8,128)} %collective-permute-done.1.refs_3_, ...), custom_call_target="tpu_custom_call" | custom-call | flops 16000000000 | bytes 8388608 | tf_op jit(solution)/shard_map/halo_rows/pallas_call | solution.py:268
  128.6 27.8 %all_to_all.15 = f32[16,96,128]{2,1,0:T(8,128)S(1)} all-to-all(f32[16,96,128]{2,1,0:T(8,128)S(1)} %bitcast.31), channel_id=1, replica_groups=mesh['x'=4,'zl'=2,'yh'=2,'yl'=2,'zh'=4,'core'=2] {'zl','yl','zh'}, dimensions={0} | all-to-all | bytes 1572864 | tf_op jit(solution)/shard_map/all_to_all | solution.py:332
  156.4 0.5 copy.8
  156.9 0.1 fusion.3
  157.1 1.2 reshape.45
  (4 shorter events, 0.0 us)
Async XLA Ops:
  0.0 1.7 %copy-start = (f32[96,2048]{1,0:T(8,128)S(1)}, f32[96,2048]{1,0:T(8,128)}, u32[]{:S(2)}) copy-start(f32[96,2048]{1,0:T(8,128)} %param.6) | copy-start | bytes 2359300
  4.5 10.1 %copy-start.1 = (f32[96,2048]{1,0:T(8,128)S(1)}, f32[96,2048]{1,0:T(8,128)}, u32[]{:S(2)}) copy-start(f32[96,2048]{1,0:T(8,128)} %param.4) | copy-start | bytes 2359300
  4.5 49.5 %all-to-all-start = ((f32[16,2,96,128]{3,2,1,0:T(8,128)}), f32[16,2,96,128]{3,2,1,0:T(8,128)S(1)}, u32[]{:S(2)}, u32[]{:S(2)}) async-start(f32[16,2,96,128]{3,2,1,0:T(8,128)} %pad_maximum_fusion), calls=%async_computation | async-start | bytes 3145728 | tf_op jit(solution)/shard_map/all_to_all | solution.py:332
  15.2 1.3 copy-start.2
  54.1 18.8 %collective-permute-start = (f32[2,2,4,2,96,128]{5,4,3,2,1,0:T(8,128)S(1)}, f32[2,2,4,2,96,128]{5,4,3,2,1,0:T(8,128)}, u32[]{:S(2)}, u32[]{:S(2)}) collective-permute-start(f32[2,2,4,2,96,128]{5,4,3,2,1,0:T(8,128)S(1)} %bitcast.25), channel_id=1, source_target_pairs={{0,1},{1,0},{2,3},{3,2},{4,5},{5,4},{6,7},{7,6},{8,9},{9,8},{10,11... | collective-permute-start | bytes 4718600 | tf_op jit(solution)/shard_map/ppermute | solution.py:335
  54.1 27.7 %all-to-all-start.1 = ((f32[16,96,128]{2,1,0:T(8,128)}), f32[16,96,128]{2,1,0:T(8,128)S(1)}, u32[]{:S(2)}, u32[]{:S(2)}) async-start(f32[16,96,128]{2,1,0:T(8,128)} %bitcast.5), calls=%async_computation.1 | async-start | bytes 1572864 | tf_op jit(solution)/shard_map/all_to_all | solution.py:332
  59.5 42.1 %collective-permute-start.5 = (f32[4,2,96,128]{3,2,1,0:T(8,128)}, f32[4,2,96,128]{3,2,1,0:T(8,128)S(1)}, u32[]{:S(2)}, u32[]{:S(2)}) collective-permute-start(f32[4,2,96,128]{3,2,1,0:T(8,128)} %get-tuple-element.29), channel_id=1, source_target_pairs={{64,24},{72,16},{80,8},{88,0},{128,88},{136,80},{144,72},{152,64},... | collective-permute-start | bytes 1179656 | tf_op jit(solution)/shard_map/ppermute | solution.py:353
  62.3 39.3 %collective-permute-start.4 = (f32[4,2,96,128]{3,2,1,0:T(8,128)}, f32[4,2,96,128]{3,2,1,0:T(8,128)}, u32[]{:S(2)}, u32[]{:S(2)}) collective-permute-start(f32[4,2,96,128]{3,2,1,0:T(8,128)} %get-tuple-element.30), channel_id=1, source_target_pairs={{0,88},{8,80},{16,72},{24,64},{64,152},{72,144},{80,136},{88,128},... | collective-permute-start | bytes 1179656 | tf_op jit(solution)/shard_map/ppermute | solution.py:352
  67.2 34.4 %collective-permute-start.3 = (f32[2,4,2,96,128]{4,3,2,1,0:T(8,128)}, f32[2,4,2,96,128]{4,3,2,1,0:T(8,128)S(1)}, u32[]{:S(2)}, u32[]{:S(2)}) collective-permute-start(f32[2,4,2,96,128]{4,3,2,1,0:T(8,128)} %dynamic-slice_bitcast_fusion), channel_id=1, source_target_pairs={{0,24},{8,16},{16,8},{24,0},{1,25},{9,17},{17,9},{25,1},{2,26},{10... | collective-permute-start | bytes 2359304 | tf_op jit(solution)/shard_map/ppermute | solution.py:349
  69.5 32.2 %collective-permute-start.1 = (f32[2,4,2,96,128]{4,3,2,1,0:T(8,128)}, f32[2,4,2,96,128]{4,3,2,1,0:T(8,128)}, u32[]{:S(2)}, u32[]{:S(2)}) collective-permute-start(f32[2,4,2,96,128]{4,3,2,1,0:T(8,128)} %bitcast.10), channel_id=1, source_target_pairs={{0,64},{64,128},{128,192},{1,65},{65,129},{129,193},{2,66},{66,130... | collective-permute-start | bytes 2359304 | tf_op jit(solution)/shard_map/ppermute | solution.py:346
  72.9 28.8 %collective-permute-start.2 = (f32[2,4,2,96,128]{4,3,2,1,0:T(8,128)}, f32[2,4,2,96,128]{4,3,2,1,0:T(8,128)}, u32[]{:S(2)}, u32[]{:S(2)}) collective-permute-start(f32[2,4,2,96,128]{4,3,2,1,0:T(8,128)} %bitcast.11), channel_id=1, source_target_pairs={{64,0},{128,64},{192,128},{65,1},{129,65},{193,129},{66,2},{130,66... | collective-permute-start | bytes 2359304 | tf_op jit(solution)/shard_map/ppermute | solution.py:347
  101.7 6.0 %collective-permute-start.6 = (f32[2,4,2,96,128]{4,3,2,1,0:T(8,128)}, f32[2,4,2,96,128]{4,3,2,1,0:T(8,128)S(1)}, u32[]{:S(2)}, u32[]{:S(2)}) collective-permute-start(f32[2,4,2,96,128]{4,3,2,1,0:T(8,128)} %collective-permute-done.1.refs_3_), channel_id=1, source_target_pairs={{0,1},{1,0},{2,3},{3,2},{4,5},{5,4},{6,7},{7,6},{8,9},{9,8},{10,11... | collective-permute-start | bytes 2359304 | tf_op jit(solution)/shard_map/ppermute | solution.py:335
  101.8 5.9 %collective-permute-start.7 = (f32[2,4,2,96,128]{4,3,2,1,0:T(8,128)}, f32[2,4,2,96,128]{4,3,2,1,0:T(8,128)S(1)}, u32[]{:S(2)}, u32[]{:S(2)}) collective-permute-start(f32[2,4,2,96,128]{4,3,2,1,0:T(8,128)} %collective-permute-done.2.refs_4_), channel_id=1, source_target_pairs={{0,1},{1,0},{2,3},{3,2},{4,5},{5,4},{6,7},{7,6},{8,9},{9,8},{10,11... | collective-permute-start | bytes 2359304 | tf_op jit(solution)/shard_map/ppermute | solution.py:335
  102.2 5.4 %collective-permute-start.8 = (f32[2,4,2,96,128]{4,3,2,1,0:T(8,128)S(1)}, f32[2,4,2,96,128]{4,3,2,1,0:T(8,128)S(1)}, u32[]{:S(2)}, u32[]{:S(2)}) collective-permute-start(f32[2,4,2,96,128]{4,3,2,1,0:T(8,128)S(1)} %collective-permute-done.3.refs_5_), channel_id=1, source_target_pairs={{0,1},{1,0},{2,3},{3,2},{4,5},{5,4},{6,7},{7,6},{8,9},{9,8},{10,11... | collective-permute-start | bytes 2359304 | tf_op jit(solution)/shard_map/ppermute | solution.py:335
  102.3 5.3 %collective-permute-start.9 = (f32[4,2,96,128]{3,2,1,0:T(8,128)}, f32[4,2,96,128]{3,2,1,0:T(8,128)S(1)}, u32[]{:S(2)}, u32[]{:S(2)}) collective-permute-start(f32[4,2,96,128]{3,2,1,0:T(8,128)} %collective-permute-done.4.refs_6_), channel_id=1, source_target_pairs={{0,1},{1,0},{2,3},{3,2},{4,5},{5,4},{6,7},{7,6},{8,9},{9,8},{10,11... | collective-permute-start | bytes 1179656 | tf_op jit(solution)/shard_map/ppermute | solution.py:335
  102.8 4.9 %collective-permute-start.10 = (f32[4,2,96,128]{3,2,1,0:T(8,128)S(1)}, f32[4,2,96,128]{3,2,1,0:T(8,128)S(1)}, u32[]{:S(2)}, u32[]{:S(2)}) collective-permute-start(f32[4,2,96,128]{3,2,1,0:T(8,128)S(1)} %collective-permute-done.5.refs_7_), channel_id=1, source_target_pairs={{0,1},{1,0},{2,3},{3,2},{4,5},{5,4},{6,7},{7,6},{8,9},{9,8},{10,11... | collective-permute-start | bytes 1179656 | tf_op jit(solution)/shard_map/ppermute | solution.py:335

commit v2 on v1

--- a/solution.py
+++ b/solution.py
@@ -20,7 +20,11 @@
 
 AXES = ("x", "zl", "yh", "yl", "zh", "core")
 SIZES = (4, 2, 2, 2, 4, 2)
-GROUP = ("zl", "yl", "zh")
+GROUP = ("yh", "zl", "yl", "zh")
+RANKS = [
+    [((yh * 2 + zl) * 2 + (yl ^ yh)) * 4 + zh for zl in range(2) for yl in range(2) for zh in range(4)]
+    for yh in range(2)
+]
 
 OWN_ROWS = ((0, 0), (0, 1), (1, 0), (1, 1))
 HALO_ROWS = ((-1, 0), (-1, 1), (2, 0), (2, 1), (0, 2), (1, 2), (-1, 2), (2, 2))
@@ -41,7 +45,7 @@
 
 
 def row_flags(rows, info):
-    in_time, in_height, in_width, x, yh = (info[i] for i in range(5))
+    in_time, in_height, in_width, x = (info[i] for i in range(4))
     one = jnp.int32(1)
     flags = []
     for t, h in rows:
@@ -51,7 +55,7 @@
             for qh in range(2):
                 near_t = one if t == qt else (in_time if abs(t - qt) == 1 else jnp.int32(0))
                 if h == 2:
-                    near_h = in_height * (yh == 1 - qh).astype(jnp.int32)
+                    near_h = in_height if qh == 1 else jnp.int32(0)
                 else:
                     near_h = one if h == qh else in_height
                 of_row.append(exists * near_t * near_h)
@@ -294,7 +298,7 @@
             pltpu.SemaphoreType.DMA((2,)),
             pltpu.SemaphoreType.DMA((2, 4)),
         ],
-        compiler_params=pltpu.CompilerParams(vmem_limit_bytes=(24 if first else 28) * 1024 * 1024),
+        compiler_params=pltpu.CompilerParams(vmem_limit_bytes=(30 if first else 34) * 1024 * 1024),
         cost_estimate=pl.CostEstimate(flops=COST, bytes_accessed=8 * 2**20, transcendentals=0),
         name="own_rows" if first else "halo_rows",
     )(info, *arrays[: 1 if first else 3], *[pltpu.with_memory_space_constraint(x, pltpu.VMEM) for x in arrays[1 if first else 3 :]])
@@ -319,17 +323,17 @@
 
 def body(queries, key_tokens, value_tokens, window_reach):
     yh = lax.axis_index("yh")
-    head = (lax.axis_index("yl") ^ yh) * 8 + lax.axis_index("zl") * 4 + lax.axis_index("zh")
+    head = lax.axis_index("zl") * 8 + (lax.axis_index("yl") ^ yh) * 4 + lax.axis_index("zh")
     reach = lax.dynamic_slice_in_dim(window_reach, head, 1, 0)[0]
-    info = jnp.concatenate([jnp.minimum(reach, 1), jnp.stack([lax.axis_index("x"), yh])])
+    info = jnp.concatenate([jnp.minimum(reach, 1), lax.axis_index("x")[None]])
 
     def pieces(tensor):
-        cut = tensor.reshape(BLOCK, 2, 2, 4, HD)
-        flipped = jnp.where(yh == 1, cut[:, ::-1], cut)
-        return flipped.transpose(2, 1, 3, 0, 4).reshape(HEADS, BLOCK, HD)
+        return tensor.reshape(BLOCK, HEADS, HD).transpose(1, 0, 2)
 
     def exchange(tensor):
-        return lax.all_to_all(tensor, GROUP, split_axis=0, concat_axis=0, tiled=True)
+        return lax.all_to_all(
+            tensor, GROUP, split_axis=0, concat_axis=0, axis_index_groups=RANKS, tiled=True
+        )
 
     def swap(tensor):
         return lax.ppermute(tensor, "core", [(0, 1), (1, 0)])
@@ -345,7 +349,7 @@
 
     xm = lax.ppermute(own[1], "x", up)
     xp = lax.ppermute(own[0], "x", down)
-    edge = lax.dynamic_index_in_dim(own, 1 - yh, 1, keepdims=False)
+    edge = own[:, 1]
     y = lax.ppermute(edge, ("yh", "yl"), across)
     edge_up = [(i * 4 + j, (i + 1) * 4 + 3 - j) for i in range(3) for j in range(4)]
     edge_down = [((i + 1) * 4 + j, i * 4 + 3 - j) for i in range(3) for j in range(4)]
@@ -356,9 +360,8 @@
     state, halo = lax.optimization_barrier((state, halo))
     halo = halo + tuple(swap(part) for part in halo)
     (out,) = attention(HALO_ROWS, halo_sources, False, info, own_q, *state, *halo)
-    back = exchange(out.reshape(HEADS, BLOCK, HD)).reshape(2, 2, 4, BLOCK, HD)
-    back = jnp.where(yh == 1, back[:, ::-1], back)
-    return back.transpose(3, 1, 0, 2, 4).reshape(BLOCK, HEADS * HD)
+    back = exchange(out.reshape(HEADS, BLOCK, HD))
+    return back.transpose(1, 0, 2).reshape(BLOCK, HEADS * HD)
 
 
 def solution(mesh):

time: 158 us -> 155 us (0.981); the launches traced: 158 us -> 157 us
  Pallas kernels: 40.8 us -> 21.8 us
  blocking collectives: 27.8 us -> 43.3 us
  waiting for transfers between devices: 47.7 us -> 52 us
  local copies, waits for them, and re-layouts: 9.39 us -> 7.59 us
    pallas_call x2, Pallas kernels: 40.8 us -> 21.8 us  [attention(): pl.pallas_call(functools.partial(attention_kernel, rows, sources, first,...]
    all_to_all x1, blocking collectives: 27.8 us -> 43.3 us  [exchange(): lax.all_to_all(tensor, GROUP, split_axis=0, concat_axis=0, axis_index_gro...]
    ppermute x1, waiting for transfers between devices: 0.01 us -> 3.95 us  [body(): y = lax.ppermute(edge, ('yh', 'yl'), across)]
    reshape x5 -> x1, local copies, waits for them, and re-layouts: 4.5 us -> 0.95 us  [body(): return back.transpose(1, 0, 2).reshape(BLOCK, HEADS * HD)]
  transfers between devices with their start and end apart: 13 -> 13, of which waited for: 3 -> 5; matrix products, arithmetic and copies ran while one was open for 3% -> 3% of each run, Pallas kernels for 13% -> 8%
where the time goes in v2:
time: 155 us; the launch traced here: 157 us
  waiting for transfers between devices  52 us (34%)
  blocking collectives  43.3 us (28%)
  starting transfers between devices  30.6 us (20%)
  Pallas kernels  21.8 us (14%)
  local copies, waits for them, and re-layouts  7.59 us (5%)
  other arithmetic  1.57 us (1%)
    all_to_all x1, blocking collectives, exchange(): lax.all_to_all(tensor, GROUP, split_axis=0, concat_axis=0, axis_index_gro...  43.3 us
    all_to_all x2, waiting for transfers between devices, exchange(): lax.all_to_all(tensor, GROUP, split_axis=0, concat_axis=0, axis_index_gro...  43.1 us
    pallas_call x2, Pallas kernels, attention(): pl.pallas_call(functools.partial(attention_kernel, rows, sources, first,...  21.8 us
    all_to_all x2, starting transfers between devices, exchange(): lax.all_to_all(tensor, GROUP, split_axis=0, concat_axis=0, axis_index_gro...  14.5 us
    ppermute x6, waiting for transfers between devices, swap(): return lax.ppermute(tensor, 'core', [(0, 1), (1, 0)])  4.8 us
    ppermute x1, waiting for transfers between devices, body(): y = lax.ppermute(edge, ('yh', 'yl'), across)  3.95 us
    ppermute x1, starting transfers between devices, body(): cp = lax.ppermute(edge[0], ('x', 'yh', 'yl'), edge_down)  3.45 us
    ppermute x1, starting transfers between devices, body(): xm = lax.ppermute(own[1], 'x', up)  3.41 us
  transfers between devices with their start and end apart: 13, of which 5 were waited for; matrix products, arithmetic and copies ran while one was open for 3% of the time, Pallas kernels for 8%

profile of v2, /device:TPU:10, one launch (start us, length us, event | category | flops | bytes accessed | tf_op | source)
XLA Modules:
  0.0 156.9 jit_solution(12418852634172461368)
XLA Ops:
  0.0 0.0 copy-start
  0.0 1.1 copy-done
  1.1 1.3 bitcast_bitcast_fusion.1
  2.5 1.3 pad_maximum_fusion
  3.8 0.0 copy-start.2
  3.8 0.0 copy-start.1
  3.8 10.1 %all-to-all-start = ((f32[16,2,96,128]{3,2,1,0:T(8,128)}), f32[16,2,96,128]{3,2,1,0:T(8,128)S(1)}, u32[]{:S(2)}, u32[]{:S(2)}) async-start(f32[16,2,96,128]{3,2,1,0:T(8,128)} %pad_maximum_fusion), calls=%async_computation | async-start | bytes 3145728 | tf_op jit(solution)/shard_map/all_to_all | solution.py:334
  13.8 0.0 copy-done.2
  13.8 0.2 minimum_reduce_fusion
  14.0 0.1 pad_add_fusion.info
  14.1 0.0 copy-done.1
  14.1 1.0 bitcast_bitcast_fusion
  15.1 38.2 %all-to-all-done = f32[16,2,96,128]{3,2,1,0:T(8,128)S(1)} async-done(((f32[16,2,96,128]{3,2,1,0:T(8,128)}), f32[16,2,96,128]{3,2,1,0:T(8,128)S(1)}, u32[]{:S(2)}, u32[]{:S(2)}) %all-to-all-start) | async-done | bytes 1572896 | tf_op jit(solution)/shard_map/all_to_all | solution.py:334
  53.3 0.0 collective-permute-start
  53.3 4.5 %all-to-all-start.1 = ((f32[16,96,128]{2,1,0:T(8,128)}), f32[16,96,128]{2,1,0:T(8,128)S(1)}, u32[]{:S(2)}, u32[]{:S(2)}) async-start(f32[16,96,128]{2,1,0:T(8,128)} %bitcast_bitcast_fusion), calls=%async_computation.1 | async-start | bytes 1572864 | tf_op jit(solution)/shard_map/all_to_all | solution.py:334
  57.8 0.9 slice_bitcast_fusion.1
  58.7 3.5 %collective-permute-start.5 = (f32[4,2,96,128]{3,2,1,0:T(8,128)}, f32[4,2,96,128]{3,2,1,0:T(8,128)S(1)}, u32[]{:S(2)}, u32[]{:S(2)}) collective-permute-start(f32[4,2,96,128]{3,2,1,0:T(8,128)} %get-tuple-element.29), channel_id=1, source_target_pairs={{64,24},{72,16},{80,8},{88,0},{128,88},{136,80},{144,72},{152,64},... | collective-permute-start | bytes 1179656 | tf_op jit(solution)/shard_map/ppermute | solution.py:357
  62.2 3.3 %collective-permute-start.4 = (f32[4,2,96,128]{3,2,1,0:T(8,128)}, f32[4,2,96,128]{3,2,1,0:T(8,128)}, u32[]{:S(2)}, u32[]{:S(2)}) collective-permute-start(f32[4,2,96,128]{3,2,1,0:T(8,128)} %get-tuple-element.30), channel_id=1, source_target_pairs={{0,88},{8,80},{16,72},{24,64},{64,152},{72,144},{80,136},{88,128},... | collective-permute-start | bytes 1179656 | tf_op jit(solution)/shard_map/ppermute | solution.py:356
  65.5 0.9 slice_bitcast_fusion
  66.4 1.6 %collective-permute-start.3 = (f32[2,4,2,96,128]{4,3,2,1,0:T(8,128)}, f32[2,4,2,96,128]{4,3,2,1,0:T(8,128)}, u32[]{:S(2)}, u32[]{:S(2)}) collective-permute-start(f32[2,4,2,96,128]{4,3,2,1,0:T(8,128)} %slice_bitcast_fusion), channel_id=1, source_target_pairs={{0,24},{8,16},{16,8},{24,0},{1,25},{9,17},{17,9},{25,1},{2,26},{10... | collective-permute-start | bytes 2359304 | tf_op jit(solution)/shard_map/ppermute | solution.py:353
  68.0 1.3 fusion
  69.3 3.4 %collective-permute-start.1 = (f32[2,4,2,96,128]{4,3,2,1,0:T(8,128)}, f32[2,4,2,96,128]{4,3,2,1,0:T(8,128)}, u32[]{:S(2)}, u32[]{:S(2)}) collective-permute-start(f32[2,4,2,96,128]{4,3,2,1,0:T(8,128)} %bitcast.8), channel_id=1, source_target_pairs={{0,64},{64,128},{128,192},{1,65},{65,129},{129,193},{2,66},{66,130... | collective-permute-start | bytes 2359304 | tf_op jit(solution)/shard_map/ppermute | solution.py:350
  72.7 0.0 collective-permute-done.refs_2_
  72.7 3.3 %collective-permute-start.2 = (f32[2,4,2,96,128]{4,3,2,1,0:T(8,128)}, f32[2,4,2,96,128]{4,3,2,1,0:T(8,128)}, u32[]{:S(2)}, u32[]{:S(2)}) collective-permute-start(f32[2,4,2,96,128]{4,3,2,1,0:T(8,128)} %bitcast.9), channel_id=1, source_target_pairs={{64,0},{128,64},{192,128},{65,1},{129,65},{193,129},{66,2},{130,66... | collective-permute-start | bytes 2359304 | tf_op jit(solution)/shard_map/ppermute | solution.py:351
  76.0 4.9 %all-to-all-done.1 = f32[16,96,128]{2,1,0:T(8,128)S(1)} async-done(((f32[16,96,128]{2,1,0:T(8,128)}), f32[16,96,128]{2,1,0:T(8,128)S(1)}, u32[]{:S(2)}, u32[]{:S(2)}) %all-to-all-start.1) | async-done | bytes 786464 | tf_op jit(solution)/shard_map/all_to_all | solution.py:334
  81.0 13.1 %own_rows.1 = (f32[4,384,128]{2,1,0:T(8,128)S(1)}, f32[4,384,128]{2,1,0:T(8,128)S(1)}) custom-call(s32[4]{0:T(128)S(1)} %pad_add_fusion.info, f32[4,384,128]{2,1,0:T(8,128)S(1)} %bitcast.47, f32[2,2,4,2,96,128]{5,4,3,2,1,0:T(8,128)S(1)} %bitcast.46, f32[2,2,4,2,96,128]{5,4,3,2,1,0:T(8,128)} %collective-permute-done.refs_2_), custom_call_target="tpu_custom_call" | custom-call | flops 16000000000 | bytes 8388608 | tf_op jit(solution)/shard_map/own_rows/pallas_call | solution.py:272
  94.1 0.0 collective-permute-done.5.refs_7_
  94.1 0.0 collective-permute-done.4.refs_6_
  94.1 4.0 %collective-permute-done.3.refs_5_ = f32[2,4,2,96,128]{4,3,2,1,0:T(8,128)} collective-permute-done((f32[2,4,2,96,128]{4,3,2,1,0:T(8,128)}, f32[2,4,2,96,128]{4,3,2,1,0:T(8,128)}, u32[]{:S(2)}, u32[]{:S(2)}) %collective-permute-start.3) | collective-permute-done | bytes 786464 | tf_op jit(solution)/shard_map/ppermute | solution.py:353
  98.0 0.1 collective-permute-done.1.refs_3_
  98.1 0.0 collective-permute-done.2.refs_4_
  98.1 0.0 collective-permute-start.6
  98.1 0.5 collective-permute-start.7
  98.6 0.1 collective-permute-start.8
  98.7 0.5 collective-permute-start.9
  99.1 0.1 collective-permute-start.10
  99.2 4.8 %collective-permute-done.9.refs_11_ = f32[4,2,96,128]{3,2,1,0:T(8,128)S(1)} collective-permute-done((f32[4,2,96,128]{3,2,1,0:T(8,128)}, f32[4,2,96,128]{3,2,1,0:T(8,128)S(1)}, u32[]{:S(2)}, u32[]{:S(2)}) %collective-permute-start.9) | collective-permute-done | bytes 393248 | tf_op jit(solution)/shard_map/ppermute | solution.py:339
  104.0 0.0 collective-permute-done.10.refs_12_
  104.0 0.0 collective-permute-done.6.refs_8_
  104.0 0.0 collective-permute-done.7.refs_9_
  104.0 0.0 collective-permute-done.8.refs_10_
  104.0 8.7 %halo_rows.1 = f32[4,384,128]{2,1,0:T(8,128)S(1)} custom-call(s32[4]{0:T(128)S(1)} %pad_add_fusion.info, f32[4,384,128]{2,1,0:T(8,128)S(1)} %bitcast.48, f32[4,384,128]{2,1,0:T(8,128)S(1)} %get-tuple-element.22.refs_1_, f32[4,384,128]{2,1,0:T(8,128)S(1)} %get-tuple-element.23.refs_2_, f32[2,4,2,96,128]{4,3,2,1,0:T(8,128)} %collective-permute-done.1.refs_3_, ...), custom_call_target="tpu_custom_call" | custom-call | flops 16000000000 | bytes 8388608 | tf_op jit(solution)/shard_map/halo_rows/pallas_call | solution.py:272
  112.7 43.3 %all_to_all.15 = f32[16,96,128]{2,1,0:T(8,128)S(1)} all-to-all(f32[16,96,128]{2,1,0:T(8,128)S(1)} %bitcast.49), channel_id=1, replica_groups={{0,2,4,6,8,10,12,14,32,34,36,38,40,42,44,46},{24,26,28,30,16,18,20,22,5..., dimensions={0} | all-to-all | bytes 1572864 | tf_op jit(solution)/shard_map/all_to_all | solution.py:334
  156.0 0.9 copy_bitcast_fusion
Async XLA Ops:
  0.0 1.1 copy-start
  3.8 10.1 %copy-start.2 = (s32[16,3]{0,1:T(4,128)S(1)}, s32[16,3]{0,1:T(4,128)}, u32[]{:S(2)}) copy-start(s32[16,3]{0,1:T(4,128)} %param.7) | copy-start | bytes 580
  3.8 10.3 %copy-start.1 = (f32[96,2048]{1,0:T(8,128)S(1)}, f32[96,2048]{1,0:T(8,128)}, u32[]{:S(2)}) copy-start(f32[96,2048]{1,0:T(8,128)} %param.4) | copy-start | bytes 2359300
  3.8 49.5 %all-to-all-start = ((f32[16,2,96,128]{3,2,1,0:T(8,128)}), f32[16,2,96,128]{3,2,1,0:T(8,128)S(1)}, u32[]{:S(2)}, u32[]{:S(2)}) async-start(f32[16,2,96,128]{3,2,1,0:T(8,128)} %pad_maximum_fusion), calls=%async_computation | async-start | bytes 3145728 | tf_op jit(solution)/shard_map/all_to_all | solution.py:334
  53.3 19.4 %collective-permute-start = (f32[2,2,4,2,96,128]{5,4,3,2,1,0:T(8,128)S(1)}, f32[2,2,4,2,96,128]{5,4,3,2,1,0:T(8,128)}, u32[]{:S(2)}, u32[]{:S(2)}) collective-permute-start(f32[2,2,4,2,96,128]{5,4,3,2,1,0:T(8,128)S(1)} %bitcast.43), channel_id=1, source_target_pairs={{0,1},{1,0},{2,3},{3,2},{4,5},{5,4},{6,7},{7,6},{8,9},{9,8},{10,11... | collective-permute-start | bytes 4718600 | tf_op jit(solution)/shard_map/ppermute | solution.py:339
  53.3 27.7 %all-to-all-start.1 = ((f32[16,96,128]{2,1,0:T(8,128)}), f32[16,96,128]{2,1,0:T(8,128)S(1)}, u32[]{:S(2)}, u32[]{:S(2)}) async-start(f32[16,96,128]{2,1,0:T(8,128)} %bitcast_bitcast_fusion), calls=%async_computation.1 | async-start | bytes 1572864 | tf_op jit(solution)/shard_map/all_to_all | solution.py:334
  58.7 35.4 %collective-permute-start.5 = (f32[4,2,96,128]{3,2,1,0:T(8,128)}, f32[4,2,96,128]{3,2,1,0:T(8,128)S(1)}, u32[]{:S(2)}, u32[]{:S(2)}) collective-permute-start(f32[4,2,96,128]{3,2,1,0:T(8,128)} %get-tuple-element.29), channel_id=1, source_target_pairs={{64,24},{72,16},{80,8},{88,0},{128,88},{136,80},{144,72},{152,64},... | collective-permute-start | bytes 1179656 | tf_op jit(solution)/shard_map/ppermute | solution.py:357
  62.2 31.9 %collective-permute-start.4 = (f32[4,2,96,128]{3,2,1,0:T(8,128)}, f32[4,2,96,128]{3,2,1,0:T(8,128)}, u32[]{:S(2)}, u32[]{:S(2)}) collective-permute-start(f32[4,2,96,128]{3,2,1,0:T(8,128)} %get-tuple-element.30), channel_id=1, source_target_pairs={{0,88},{8,80},{16,72},{24,64},{64,152},{72,144},{80,136},{88,128},... | collective-permute-start | bytes 1179656 | tf_op jit(solution)/shard_map/ppermute | solution.py:356
  66.4 31.7 %collective-permute-start.3 = (f32[2,4,2,96,128]{4,3,2,1,0:T(8,128)}, f32[2,4,2,96,128]{4,3,2,1,0:T(8,128)}, u32[]{:S(2)}, u32[]{:S(2)}) collective-permute-start(f32[2,4,2,96,128]{4,3,2,1,0:T(8,128)} %slice_bitcast_fusion), channel_id=1, source_target_pairs={{0,24},{8,16},{16,8},{24,0},{1,25},{9,17},{17,9},{25,1},{2,26},{10... | collective-permute-start | bytes 2359304 | tf_op jit(solution)/shard_map/ppermute | solution.py:353
  69.3 28.8 %collective-permute-start.1 = (f32[2,4,2,96,128]{4,3,2,1,0:T(8,128)}, f32[2,4,2,96,128]{4,3,2,1,0:T(8,128)}, u32[]{:S(2)}, u32[]{:S(2)}) collective-permute-start(f32[2,4,2,96,128]{4,3,2,1,0:T(8,128)} %bitcast.8), channel_id=1, source_target_pairs={{0,64},{64,128},{128,192},{1,65},{65,129},{129,193},{2,66},{66,130... | collective-permute-start | bytes 2359304 | tf_op jit(solution)/shard_map/ppermute | solution.py:350
  72.7 25.4 %collective-permute-start.2 = (f32[2,4,2,96,128]{4,3,2,1,0:T(8,128)}, f32[2,4,2,96,128]{4,3,2,1,0:T(8,128)}, u32[]{:S(2)}, u32[]{:S(2)}) collective-permute-start(f32[2,4,2,96,128]{4,3,2,1,0:T(8,128)} %bitcast.9), channel_id=1, source_target_pairs={{64,0},{128,64},{192,128},{65,1},{129,65},{193,129},{66,2},{130,66... | collective-permute-start | bytes 2359304 | tf_op jit(solution)/shard_map/ppermute | solution.py:351
  98.1 5.9 %collective-permute-start.6 = (f32[2,4,2,96,128]{4,3,2,1,0:T(8,128)}, f32[2,4,2,96,128]{4,3,2,1,0:T(8,128)S(1)}, u32[]{:S(2)}, u32[]{:S(2)}) collective-permute-start(f32[2,4,2,96,128]{4,3,2,1,0:T(8,128)} %collective-permute-done.1.refs_3_), channel_id=1, source_target_pairs={{0,1},{1,0},{2,3},{3,2},{4,5},{5,4},{6,7},{7,6},{8,9},{9,8},{10,11... | collective-permute-start | bytes 2359304 | tf_op jit(solution)/shard_map/ppermute | solution.py:339
  98.1 5.9 %collective-permute-start.7 = (f32[2,4,2,96,128]{4,3,2,1,0:T(8,128)}, f32[2,4,2,96,128]{4,3,2,1,0:T(8,128)S(1)}, u32[]{:S(2)}, u32[]{:S(2)}) collective-permute-start(f32[2,4,2,96,128]{4,3,2,1,0:T(8,128)} %collective-permute-done.2.refs_4_), channel_id=1, source_target_pairs={{0,1},{1,0},{2,3},{3,2},{4,5},{5,4},{6,7},{7,6},{8,9},{9,8},{10,11... | collective-permute-start | bytes 2359304 | tf_op jit(solution)/shard_map/ppermute | solution.py:339
  98.6 5.4 %collective-permute-start.8 = (f32[2,4,2,96,128]{4,3,2,1,0:T(8,128)}, f32[2,4,2,96,128]{4,3,2,1,0:T(8,128)S(1)}, u32[]{:S(2)}, u32[]{:S(2)}) collective-permute-start(f32[2,4,2,96,128]{4,3,2,1,0:T(8,128)} %collective-permute-done.3.refs_5_), channel_id=1, source_target_pairs={{0,1},{1,0},{2,3},{3,2},{4,5},{5,4},{6,7},{7,6},{8,9},{9,8},{10,11... | collective-permute-start | bytes 2359304 | tf_op jit(solution)/shard_map/ppermute | solution.py:339
  98.7 5.3 %collective-permute-start.9 = (f32[4,2,96,128]{3,2,1,0:T(8,128)}, f32[4,2,96,128]{3,2,1,0:T(8,128)S(1)}, u32[]{:S(2)}, u32[]{:S(2)}) collective-permute-start(f32[4,2,96,128]{3,2,1,0:T(8,128)} %collective-permute-done.4.refs_6_), channel_id=1, source_target_pairs={{0,1},{1,0},{2,3},{3,2},{4,5},{5,4},{6,7},{7,6},{8,9},{9,8},{10,11... | collective-permute-start | bytes 1179656 | tf_op jit(solution)/shard_map/ppermute | solution.py:339
  99.1 4.9 %collective-permute-start.10 = (f32[4,2,96,128]{3,2,1,0:T(8,128)S(1)}, f32[4,2,96,128]{3,2,1,0:T(8,128)S(1)}, u32[]{:S(2)}, u32[]{:S(2)}) collective-permute-start(f32[4,2,96,128]{3,2,1,0:T(8,128)S(1)} %collective-permute-done.5.refs_7_), channel_id=1, source_target_pairs={{0,1},{1,0},{2,3},{3,2},{4,5},{5,4},{6,7},{7,6},{8,9},{9,8},{10,11... | collective-permute-start | bytes 1179656 | tf_op jit(solution)/shard_map/ppermute | solution.py:339
